TPU v7x, 32 devices: a whole 2x2x4 slice. The times are simulated.
32 devices in a mesh: dp: 8 (over z, y), pipe: 4 (over x, core).
Axes of the slice: x: 2, y: 2, z: 4, core: 2. Of those that a mesh axis runs over, the one named last changes fastest.
Arguments:
- numeric: float32 [8192, 128], P('dp'), may hold values from -6 to 6
- categories: int32 [8192, 24], P('dp'), may hold values from 0 to 255, as said below
- cardinalities: int32 [24], replicated, may hold values from 64 to 256, as said below
- embed_table: bfloat16 [24, 256, 16], replicated, may hold values from -6 to 6
- bn_gain: float32 [2, 512], replicated, may hold values from 0.25 to 1.75
- bn_bias: float32 [2, 512], replicated, may hold values from -3 to 3
- mask_logits: float32 [12, 512], P('pipe'), may hold values from -5 to 5
- feature_allow: int32 [12, 512], P('pipe'), may hold values from 0 to 1, as said below
- gate_weight: bfloat16 [12, 1024, 1024], P('pipe'), may hold values from -0.1875 to 0.1875
- gate_bias: float32 [12, 1024], P('pipe'), may hold values from -3 to 3
- cand_weight: bfloat16 [12, 1024, 512], P('pipe'), may hold values from -0.1875 to 0.1875
- cand_bias: float32 [12, 512], P('pipe'), may hold values from -3 to 3
- out_grad: float32 [8192, 512], P('dp'), may hold values from -6 to 6
Outputs:
- block_out: float32 [8192, 512], P('dp', 'pipe')
- numeric_grad: float32 [8192, 128], P('dp', 'pipe')
- table_grad: float32 [24, 256, 16], replicated
- gain_grad: float32 [2, 512], replicated
- bias_grad: float32 [2, 512], replicated
- logit_grad: float32 [12, 512], P('pipe')
- gate_weight_grad: float32 [12, 1024, 1024], P('pipe')
- gate_bias_grad: float32 [12, 1024], P('pipe')
- cand_weight_grad: float32 [12, 1024, 512], P('pipe')
- cand_bias_grad: float32 [12, 512], P('pipe')
Inputs may be any that keep to these rules, and one draw needn't show every extreme that they name: categories[r, c] is below cardinalities[c]. `cardinalities`: some column has exactly 256 categories. `feature_allow`: every segment allows at least one feature.
All inputs are finite; a program needn't handle non-finite values.
Results may differ from a plain program's by a relative error of at most 0.0128.
The roundings to bfloat16 on the way count: a program that leaves them out, or rounds other values in their place, can miss the bound.
Values may be sent and summed in bfloat16 or wider, within the bound.
No kernel may reach another device: no remote copies, remote signals or barrier semaphores. Data moves between devices by JAX's collectives and lax.ppermute only.
A program may use at most 192 MiB of HBM per device.

v0:
```python
import jax
import jax.numpy as jnp
from jax import lax
from jax.sharding import PartitionSpec as P

MB = 8
ROWS_MB = 128


eps_norm = 1e-05


def passed_along(value, axis, by):
    length = lax.axis_size(axis)
    pairs = [(i, i + by) for i in range(length) if 0 <= i + by < length]
    return lax.ppermute(value, axis, pairs)


def feature_share(logits, allow):
    allowed = allow > 0
    largest = jnp.max(jnp.where(allowed, logits, -1e30), axis=-1, keepdims=True)
    raised = jnp.where(allowed, jnp.exp(jnp.where(allowed, logits - largest, 0.0)), 0.0)
    return raised / jnp.sum(raised, axis=-1, keepdims=True)


def one_hot_rows(category_rows, column_sizes, level_count):
    levels = jnp.arange(level_count, dtype=jnp.int32)
    matches = (category_rows[:, :, None] == levels) & (levels < column_sizes[:, None])
    return matches.astype(jnp.bfloat16)


def gated_forward(hidden, inputs, scale, w_gate, b_gate, w_cand, b_cand):
    hidden_width = hidden.shape[1]
    masked = (inputs * scale).astype(jnp.bfloat16)
    gate_input = jnp.concatenate([hidden.astype(jnp.bfloat16), masked], axis=1)
    gate_pre = jnp.dot(gate_input, w_gate, preferred_element_type=jnp.float32) + b_gate
    update_gate = jax.nn.sigmoid(gate_pre[:, :hidden_width])
    reset_gate = jax.nn.sigmoid(gate_pre[:, hidden_width:])
    cand_input = jnp.concatenate([(reset_gate * hidden).astype(jnp.bfloat16), masked], axis=1)
    candidate = jnp.tanh(jnp.dot(cand_input, w_cand, preferred_element_type=jnp.float32) + b_cand)
    result = (1.0 - update_gate) * hidden + update_gate * candidate
    return (result, (gate_input, cand_input, update_gate, reset_gate, candidate))


def gated_backward(grad_out, hidden, inputs, scale, w_gate, w_cand, saved):
    gate_input, cand_input, update_gate, reset_gate, candidate = saved
    hidden_width = hidden.shape[1]
    rows_dims = (((1,), (1,)), ((), ()))
    grad_update = grad_out * (candidate - hidden)
    grad_cand = (grad_out * update_gate * (1.0 - candidate * candidate)).astype(jnp.bfloat16)
    grad_hidden = grad_out * (1.0 - update_gate)
    back_cand = lax.dot_general(grad_cand, w_cand, rows_dims, preferred_element_type=jnp.float32)
    grad_reset_hidden = back_cand[:, :hidden_width]
    grad_masked = back_cand[:, hidden_width:]
    grad_hidden = grad_hidden + grad_reset_hidden * reset_gate
    grad_reset = grad_reset_hidden * hidden
    grad_gate = jnp.concatenate(
        [
            grad_update * update_gate * (1.0 - update_gate),
            grad_reset * reset_gate * (1.0 - reset_gate),
        ],
        axis=1,
    ).astype(jnp.bfloat16)
    back_gate = lax.dot_general(grad_gate, w_gate, rows_dims, preferred_element_type=jnp.float32)
    grad_hidden = grad_hidden + back_gate[:, :hidden_width]
    grad_masked = grad_masked + back_gate[:, hidden_width:]
    grad_scale = jnp.sum(grad_masked * inputs, axis=0)
    input_gradients = grad_masked * scale
    return (grad_hidden, input_gradients, grad_scale, grad_gate, grad_cand)


def weight_terms(gate_input, cand_input, grad_gate, grad_cand):
    contract = (((0,), (0,)), ((), ()))
    gate_term = lax.dot_general(gate_input, grad_gate, contract, preferred_element_type=jnp.float32)
    cand_term = lax.dot_general(cand_input, grad_cand, contract, preferred_element_type=jnp.float32)
    return (
        gate_term,
        jnp.sum(grad_gate.astype(jnp.float32), axis=0),
        cand_term,
        jnp.sum(grad_cand.astype(jnp.float32), axis=0),
    )


def on_device(
    numeric,
    categories,
    cardinalities,
    embed_table,
    bn_gain,
    bn_bias,
    mask_logits,
    feature_allow,
    gate_weight,
    gate_bias,
    cand_weight,
    cand_bias,
    out_grad,
):
    pipe_count = lax.axis_size("pipe")
    pipe_rank = lax.axis_index("pipe")
    layer_span = pipe_count // 2
    starts_layer = pipe_rank % layer_span == 0
    layer_index = pipe_rank // layer_span
    first_rank = pipe_rank == 0
    last_rank = pipe_rank == pipe_count - 1
    tick_count = MB + pipe_count - 1
    feature_width = out_grad.shape[1]
    numeric_width = numeric.shape[1]
    column_count = categories.shape[1]
    level_count = embed_table.shape[1]
    embed_width = embed_table.shape[2]
    local_segments = gate_weight.shape[0]
    normalized_rows = ROWS_MB * lax.axis_size("dp")
    norm_gain = lax.dynamic_index_in_dim(bn_gain, layer_index, 0, keepdims=False)
    norm_bias = lax.dynamic_index_in_dim(bn_bias, layer_index, 0, keepdims=False)
    layer_pick = (jnp.arange(2) == layer_index).astype(jnp.float32)[:, None]
    shares = feature_share(mask_logits, feature_allow)
    scales = feature_width * shares
    numeric_blocks = numeric.reshape(MB, ROWS_MB, numeric_width)
    category_blocks = categories.reshape(MB, ROWS_MB, column_count)
    cotangent_blocks = out_grad.reshape(MB, ROWS_MB, feature_width)

    def moments(source):
        total_sum = lax.psum(jnp.sum(source, axis=0), "dp")
        average = total_sum / normalized_rows
        centred = source - average
        variance = lax.psum(jnp.sum(centred * centred, axis=0), "dp") / normalized_rows
        return (average, lax.rsqrt(variance + eps_norm))

    def stored_at(store, batch_position, is_live, value):
        return store.at[batch_position].set(jnp.where(is_live, value, store[batch_position]))

    row_shape = (ROWS_MB, feature_width)
    forward_start = (
        jnp.zeros(row_shape, jnp.bfloat16),
        jnp.zeros(row_shape, jnp.bfloat16),
        jnp.zeros((MB,) + row_shape, jnp.float32),
        jnp.zeros((MB,) + row_shape, jnp.float32),
        jnp.zeros((MB, local_segments) + row_shape, jnp.float32),
        jnp.zeros((MB, feature_width), jnp.float32),
        jnp.zeros((MB, feature_width), jnp.float32),
        jnp.zeros((MB,) + row_shape, jnp.float32),
    )

    def forward_tick(carried, clock_step):
        (
            recv_hidden,
            recv_inputs,
            retained_source,
            keep_inputs,
            keep_hidden,
            retained_average,
            keep_spread,
            keep_output,
        ) = carried
        micro_batch = clock_step - pipe_rank
        is_live = (micro_batch >= 0) & (micro_batch < MB)
        batch_position = jnp.clip(micro_batch, 0, MB - 1)
        onehot = one_hot_rows(category_blocks[batch_position], cardinalities, level_count)
        embedded = jnp.einsum(
            "rcv,cve->rce", onehot, embed_table, preferred_element_type=jnp.float32
        )
        own_rows = jnp.concatenate(
            [numeric_blocks[batch_position], embedded.reshape(ROWS_MB, column_count * embed_width)],
            axis=1,
        )
        received = recv_hidden.astype(jnp.float32)
        source = jnp.where(first_rank, own_rows, received)
        average, spread_width = moments(source)
        normed = (source - average) * spread_width * norm_gain + norm_bias
        inputs = jnp.where(starts_layer, normed, recv_inputs.astype(jnp.float32))
        hidden = jnp.where(starts_layer, 0.0, received)
        segment_states = []
        for k in range(local_segments):
            segment_states.append(hidden)
            hidden, unused = gated_forward(
                hidden,
                inputs,
                scales[k],
                gate_weight[k],
                gate_bias[k],
                cand_weight[k],
                cand_bias[k],
            )
        next_hidden, next_inputs = passed_along(
            (hidden.astype(jnp.bfloat16), inputs.astype(jnp.bfloat16)), "pipe", 1
        )
        retained_source = stored_at(retained_source, batch_position, is_live, source)
        keep_inputs = stored_at(keep_inputs, batch_position, is_live, inputs)
        keep_hidden = stored_at(keep_hidden, batch_position, is_live, jnp.stack(segment_states))
        retained_average = stored_at(retained_average, batch_position, is_live, average)
        keep_spread = stored_at(keep_spread, batch_position, is_live, spread_width)
        keep_output = stored_at(keep_output, batch_position, is_live, hidden)
        return (
            (
                next_hidden,
                next_inputs,
                retained_source,
                keep_inputs,
                keep_hidden,
                retained_average,
                keep_spread,
                keep_output,
            ),
            None,
        )

    forward_end, unused = lax.scan(forward_tick, forward_start, jnp.arange(tick_count))
    retained_source, keep_inputs, keep_hidden, retained_average, keep_spread, keep_output = (
        forward_end[2:]
    )
    double_width = 2 * feature_width
    segment_store = (
        jnp.zeros((local_segments, double_width, double_width), jnp.float32),
        jnp.zeros((local_segments, double_width), jnp.float32),
        jnp.zeros((local_segments, double_width, feature_width), jnp.float32),
        jnp.zeros((local_segments, feature_width), jnp.float32),
    )
    backward_start = (
        jnp.zeros(row_shape, jnp.bfloat16),
        jnp.zeros(row_shape, jnp.bfloat16),
        segment_store,
        jnp.zeros((local_segments, feature_width), jnp.float32),
        jnp.zeros((2, feature_width), jnp.float32),
        jnp.zeros((2, feature_width), jnp.float32),
        jnp.zeros((MB,) + row_shape, jnp.float32),
    )

    def backward_tick(carried, clock_step):
        (
            recv_grad_hidden,
            recv_grad_inputs,
            segment_store,
            scale_acc,
            gain_acc,
            bias_acc,
            feature_store,
        ) = carried
        micro_batch = MB - 1 - (clock_step - (pipe_count - 1 - pipe_rank))
        is_live = (micro_batch >= 0) & (micro_batch < MB)
        batch_position = jnp.clip(micro_batch, 0, MB - 1)
        grad_hidden = jnp.where(
            last_rank, cotangent_blocks[batch_position], recv_grad_hidden.astype(jnp.float32)
        )
        input_gradients = recv_grad_inputs.astype(jnp.float32)
        inputs = keep_inputs[batch_position]
        store_parts = list(segment_store)
        for k in reversed(range(local_segments)):
            hidden = keep_hidden[batch_position, k]
            unused, saved = gated_forward(
                hidden,
                inputs,
                scales[k],
                gate_weight[k],
                gate_bias[k],
                cand_weight[k],
                cand_bias[k],
            )
            grad_hidden, grad_more, grad_scale, grad_gate, grad_cand = gated_backward(
                grad_hidden, hidden, inputs, scales[k], gate_weight[k], cand_weight[k], saved
            )
            input_gradients = input_gradients + grad_more
            scale_acc = scale_acc.at[k].add(jnp.where(is_live, grad_scale, 0.0))
            terms = weight_terms(saved[0], saved[1], grad_gate, grad_cand)
            for p in range(4):
                store_parts[p] = store_parts[p].at[k].add(jnp.where(is_live, terms[p], 0.0))
        spread_width = keep_spread[batch_position]
        normalized_input = (
            retained_source[batch_position] - retained_average[batch_position]
        ) * spread_width
        local_sum = jnp.sum(input_gradients, axis=0)
        local_cross_term = jnp.sum(input_gradients * normalized_input, axis=0)
        gradient_total, cross_gradient = lax.psum((local_sum, local_cross_term), "dp")
        grad_source = (
            norm_gain
            * spread_width
            * (
                input_gradients
                - gradient_total / normalized_rows
                - normalized_input * cross_gradient / normalized_rows
            )
        )
        live_norm = is_live & starts_layer
        gain_acc = gain_acc + jnp.where(live_norm, layer_pick * local_cross_term, 0.0)
        bias_acc = bias_acc + jnp.where(live_norm, layer_pick * local_sum, 0.0)
        live_first = is_live & first_rank
        feature_store = stored_at(feature_store, batch_position, live_first, grad_source)
        send_hidden = jnp.where(starts_layer, grad_source, grad_hidden).astype(jnp.bfloat16)
        send_inputs = jnp.where(starts_layer, 0.0, input_gradients).astype(jnp.bfloat16)
        prior_hidden, prior_inputs = passed_along((send_hidden, send_inputs), "pipe", -1)
        return (
            (
                prior_hidden,
                prior_inputs,
                tuple(store_parts),
                scale_acc,
                gain_acc,
                bias_acc,
                feature_store,
            ),
            None,
        )

    backward_end, unused = lax.scan(backward_tick, backward_start, jnp.arange(tick_count))
    unused_hidden, unused_inputs, segment_store, scale_acc, gain_acc, bias_acc, feature_store = (
        backward_end
    )
    scaled_grads = feature_width * scale_acc
    logit_local = shares * (scaled_grads - jnp.sum(shares * scaled_grads, axis=-1, keepdims=True))
    gate_w_grad, gate_b_grad, cand_w_grad, cand_b_grad, logit_total = lax.psum(
        (segment_store[0], segment_store[1], segment_store[2], segment_store[3], logit_local), "dp"
    )
    local_rows = MB * ROWS_MB
    embedded_width = column_count * embed_width
    out_terms = jnp.where(last_rank, keep_output, 0.0).reshape(local_rows, feature_width)
    flat_features = feature_store.reshape(local_rows, feature_width)
    numeric_terms = flat_features[:, :numeric_width]
    embed_terms = flat_features[:, numeric_width:]
    block_part, numeric_part, embed_part = (
        lax.psum_scatter(out_terms, "pipe", scatter_dimension=1, tiled=True),
        lax.psum_scatter(numeric_terms, "pipe", scatter_dimension=1, tiled=True),
        lax.psum_scatter(embed_terms, "pipe", scatter_dimension=1, tiled=True),
    )
    share_width = embed_part.shape[1]
    placed = lax.dynamic_update_slice(
        jnp.zeros((local_rows, embedded_width), jnp.bfloat16),
        embed_part.astype(jnp.bfloat16),
        (jnp.int32(0), pipe_rank * share_width),
    )
    onehot_all = one_hot_rows(categories, cardinalities, level_count)
    table_term = jnp.einsum(
        "rcv,rce->cve",
        onehot_all,
        placed.reshape(local_rows, column_count, embed_width),
        preferred_element_type=jnp.float32,
    )
    table_total, gain_total, bias_total = lax.psum((table_term, gain_acc, bias_acc), ("dp", "pipe"))
    return (
        block_part,
        numeric_part,
        table_total,
        gain_total,
        bias_total,
        logit_total,
        gate_w_grad,
        gate_b_grad,
        cand_w_grad,
        cand_b_grad,
    )


def solution(mesh):
    in_specs = (
        P("dp", None),
        P("dp", None),
        P(),
        P(),
        P(),
        P(),
        P("pipe", None),
        P("pipe", None),
        P("pipe", None, None),
        P("pipe", None),
        P("pipe", None, None),
        P("pipe", None),
        P("dp", None),
    )
    out_specs = (
        P("dp", "pipe"),
        P("dp", "pipe"),
        P(),
        P(),
        P(),
        P("pipe", None),
        P("pipe", None, None),
        P("pipe", None),
        P("pipe", None, None),
        P("pipe", None),
    )
    return jax.shard_map(
        on_device, mesh=mesh, in_specs=in_specs, out_specs=out_specs, check_vma=False
    )
```

profile of v0, /device:TPU:1, one launch (start us, length us, event | category | flops | bytes accessed | tf_op | source)
XLA Modules:
  0.0 2692.2 jit_solution(12012920665991353145)
XLA Ops:
  22.7 809.4 %while.78 = (s32[]{:T(128)}, bf16[128,512]{1,0:T(8,128)(2,1)S(1)}, bf16[128,512]{1,0:T(8,128)(2,1)}, f32[8,128,512]{2,1,0:T(8,128)S(1)}, f32[8,128,512]{2,1,0:T(...) while((s32[]{:T(128)}, bf16[128,512]{1,0:T(8,128)(2,1)S(1)}, ...), condition=%wide.region_10.11_spmd, body=%wide.region_2.10_spmd.sunk | while | flops 1244276224 | bytes 53673708 | solution.py:208
  28.5 18.7 psum.104
  47.3 13.7 psum.105
  76.4 11.1 collective-permute-start
  106.8 15.4 psum.104
  122.2 13.8 psum.105
  151.4 9.1 collective-permute-start
  179.9 15.4 psum.104
  195.3 13.8 psum.105
  224.5 9.2 collective-permute-start
  253.0 15.4 psum.104
  268.4 13.8 psum.105
  297.6 9.2 collective-permute-start
  326.1 15.4 psum.104
  341.6 13.8 psum.105
  370.8 9.2 collective-permute-start
  399.2 15.4 psum.104
  414.7 13.8 psum.105
  443.9 9.2 collective-permute-start
  472.3 15.4 psum.104
  487.8 13.8 psum.105
  517.0 9.1 collective-permute-start
  545.5 15.4 psum.104
  560.9 13.8 psum.105
  590.1 9.1 collective-permute-start
  618.5 15.4 psum.104
  634.0 13.8 psum.105
  663.2 9.2 collective-permute-start
  691.7 15.4 psum.104
  707.2 13.8 psum.105
  736.3 9.2 collective-permute-start
  764.8 15.4 psum.104
  780.3 13.8 psum.105
  809.5 9.1 collective-permute-start
  834.0 6.4 broadcast_in_dim.115
  847.2 1013.5 %while.79 = (s32[]{:T(128)}, bf16[128,512]{1,0:T(8,128)(2,1)}, bf16[128,512]{1,0:T(8,128)(2,1)}, f32[3,1024,1024]{2,1,0:T(8,128)}, f32[3,1024]{1,0:T(4,128)}, /*...) while((s32[]{:T(128)}, bf16[128,512]{1,0:T(8,128)(2,1)}, ...), condition=%wide.region_27.28_spmd.clone, body=%wide.region_12.27_spmd.clone.sunk | while | flops 3657382912 | bytes 150350960 | solution.py:304
  882.0 16.1 all-reduce.5
  900.7 6.8 collective-permute-start.2
  977.2 14.6 all-reduce.5
  1002.3 5.0 fusion.356
  1068.0 16.1 all-reduce.5
  1160.8 14.6 all-reduce.5
  1186.0 5.0 fusion.356
  1251.7 16.1 all-reduce.5
  1278.9 5.0 fusion.356
  1344.5 14.6 all-reduce.5
  1369.7 5.0 fusion.356
  1435.4 16.1 all-reduce.5
  1462.5 5.0 fusion.356
  1528.2 14.6 all-reduce.5
  1553.4 5.0 fusion.356
  1619.0 16.0 all-reduce.5
  1646.2 5.0 fusion.356
  1711.8 14.6 all-reduce.5
  1737.1 5.0 fusion.356
  1802.7 16.0 all-reduce.5
  1866.3 36.6 %reduce-scatter.8.cloned.1.call-done = f32[1024,96]{0,1:T(8,128)} async-done(((f32[1024,384]{0,1:T(8,128)}), f32[1024,96]{0,1:T(8,128)}) %reduce-scatter.8.cloned.1.call-update) | async-done | bytes 393232 | tf_op jit(solution)/shard_map/reduce_scatter | solution.py:322
  1904.0 7.9 fusion.204
  1914.5 39.8 %all-reduce.1 = (f32[2,512]{1,0:T(2,128)}, f32[2,512]{1,0:T(2,128)}) all-reduce(f32[2,512]{1,0:T(2,128)S(1)} %copy-done.51, f32[2,512]{1,0:T(2,128)S(1)} %copy-done.54), channel_id=1, replica_groups=mesh['dp'=8,'pipe'=4] {'dp','pipe'}, use_global_device_ids=true, to_apply=%region_31.32 | all-reduce | flops 2048 | bytes 16384 | tf_op jit(solution)/shard_map/psum | solution.py:337
  1954.4 29.4 %all-reduce.2 = (f32[3,512]{1,0:T(4,128)}, f32[3,1024]{1,0:T(4,128)}, f32[3,512]{1,0:T(4,128)}) all-reduce(f32[3,512]{1,0:T(4,128)S(1)} %subtract_multiply_fusion.1, f32[3,1024]{1,0:T(4,128)S(1)} %copy-done.33, f32[3,512]{1,0:T(4,128)S(1)} %copy-done.44), channel_id=1, replica_groups=mesh['dp'=8,'pipe'=4] {'dp'}, use_global_device_ids=true, to_apply=%region_34.35 | all-reduce | flops 6144 | bytes 49152 | tf_op jit(solution)/shard_map/psum | solution.py:310
  1983.9 76.6 %all-reduce.9.cloned.1.call-done = f32[24,256,16]{1,2,0:T(8,128)} async-done(((f32[24,256,16]{1,2,0:T(8,128)}), f32[24,256,16]{1,2,0:T(8,128)}) %all-reduce.9.cloned.1.call-update) | async-done | bytes 393232 | tf_op jit(solution)/shard_map/psum | solution.py:337
  2060.4 35.0 %reduce-scatter.4.cloned.1.call-done = f32[1024,128]{1,0:T(8,128)} async-done(((f32[1024,512]{1,0:T(8,128)}), f32[1024,128]{1,0:T(8,128)}) %reduce-scatter.4.cloned.1.call-update) | async-done | bytes 524304 | tf_op jit(solution)/shard_map/reduce_scatter | solution.py:320
  2095.4 573.4 %all-reduce.11.cloned.1.call-done = (f32[3,1024,1024]{2,1,0:T(8,128)}, f32[3,1024,512]{2,1,0:T(8,128)}) async-done(((f32[3,1024,1024]{2,1,0:T(8,128)}, f32[3,1024,512]{2,1,0:T(8,128)}), (f32[3,1024,1024]{2,1,0:T(8,128)}, f32[3,1024,512]{2,1,0:T(8,128)})) %all-reduce.11.cloned.1.call-update) | async-done | bytes 18874384 | tf_op jit(solution)/shard_map/psum | solution.py:310
  2670.7 12.2 copy.122
  (2520 shorter events, 1192.6 us)
Async XLA Ops:
  7.2 1895.7 %reduce-scatter.8.cloned.1.call-start = ((), (), s32[]{:S(2)}) async-start(), calls=%async_computation.5 | async-start | bytes 1966080 | tf_op jit(solution)/shard_map/reduce_scatter | solution.py:322
  74.2 26.8 copy-start.68
  76.4 24.5 collective-permute-start
  87.5 13.5 collective-permute-start.1
  151.4 22.6 collective-permute-start
  160.6 13.5 collective-permute-start.1
  222.3 24.9 copy-start.68
  224.5 22.7 collective-permute-start
  233.7 13.5 collective-permute-start.1
  295.4 24.9 copy-start.68
  297.6 22.6 collective-permute-start
  306.8 13.5 collective-permute-start.1
  368.5 24.9 copy-start.68
  370.8 22.6 collective-permute-start
  379.9 13.5 collective-permute-start.1
  441.6 24.9 copy-start.68
  443.9 22.6 collective-permute-start
  453.0 13.5 collective-permute-start.1
  514.7 24.9 copy-start.68
  517.0 22.6 collective-permute-start
  526.1 13.5 collective-permute-start.1
  587.8 24.9 copy-start.68
  590.1 22.6 collective-permute-start
  599.2 13.5 collective-permute-start.1
  660.9 24.9 copy-start.68
  663.2 22.7 collective-permute-start
  672.4 13.5 collective-permute-start.1
  734.1 24.9 copy-start.68
  736.3 22.7 collective-permute-start
  745.5 13.5 collective-permute-start.1
  807.2 24.9 copy-start.68
  809.5 22.6 collective-permute-start
  818.6 13.5 collective-permute-start.1
  900.7 41.1 %collective-permute-start.2 = (bf16[128,512]{1,0:T(8,128)(2,1)}, bf16[128,512]{1,0:T(8,128)(2,1)}, u32[]{:S(2)}, u32[]{:S(2)}) collective-permute-start(bf16[128,512]{1,0:T(8,128)(2,1)} %fusion.355), channel_id=1, source_target_pairs={{1,0},{2,1},{3,2},{5,4},{6,5},{7,6},{9,8},{10,9},{11,10},{13,12},{... | collective-permute-start | bytes 393224 | tf_op jit(solution)/shard_map/while/body/eval_jaxpr/ppermute | solution.py:16
  907.5 34.4 %collective-permute-start.3 = (bf16[128,512]{1,0:T(8,128)(2,1)}, bf16[128,512]{1,0:T(8,128)(2,1)}, u32[]{:S(2)}, u32[]{:S(2)}) collective-permute-start(bf16[128,512]{1,0:T(8,128)(2,1)} %get-tuple-element.1667), channel_id=1, source_target_pairs={{1,0},{2,1},{3,2},{5,4},{6,5},{7,6},{9,8},{10,9},{11,10},{13,12},{... | collective-permute-start | bytes 393224 | tf_op jit(solution)/shard_map/while/body/eval_jaxpr/ppermute | solution.py:16
  994.4 38.3 %collective-permute-start.2 = (bf16[128,512]{1,0:T(8,128)(2,1)}, bf16[128,512]{1,0:T(8,128)(2,1)}, u32[]{:S(2)}, u32[]{:S(2)}) collective-permute-start(bf16[128,512]{1,0:T(8,128)(2,1)} %fusion.355), channel_id=1, source_target_pairs={{1,0},{2,1},{3,2},{5,4},{6,5},{7,6},{9,8},{10,9},{11,10},{13,12},{... | collective-permute-start | bytes 393224 | tf_op jit(solution)/shard_map/while/body/eval_jaxpr/ppermute | solution.py:16
  998.3 34.4 %collective-permute-start.3 = (bf16[128,512]{1,0:T(8,128)(2,1)}, bf16[128,512]{1,0:T(8,128)(2,1)}, u32[]{:S(2)}, u32[]{:S(2)}) collective-permute-start(bf16[128,512]{1,0:T(8,128)(2,1)} %get-tuple-element.1667), channel_id=1, source_target_pairs={{1,0},{2,1},{3,2},{5,4},{6,5},{7,6},{9,8},{10,9},{11,10},{13,12},{... | collective-permute-start | bytes 393224 | tf_op jit(solution)/shard_map/while/body/eval_jaxpr/ppermute | solution.py:16
  1086.7 38.8 %collective-permute-start.2 = (bf16[128,512]{1,0:T(8,128)(2,1)}, bf16[128,512]{1,0:T(8,128)(2,1)}, u32[]{:S(2)}, u32[]{:S(2)}) collective-permute-start(bf16[128,512]{1,0:T(8,128)(2,1)} %fusion.355), channel_id=1, source_target_pairs={{1,0},{2,1},{3,2},{5,4},{6,5},{7,6},{9,8},{10,9},{11,10},{13,12},{... | collective-permute-start | bytes 393224 | tf_op jit(solution)/shard_map/while/body/eval_jaxpr/ppermute | solution.py:16
  1091.1 34.4 %collective-permute-start.3 = (bf16[128,512]{1,0:T(8,128)(2,1)}, bf16[128,512]{1,0:T(8,128)(2,1)}, u32[]{:S(2)}, u32[]{:S(2)}) collective-permute-start(bf16[128,512]{1,0:T(8,128)(2,1)} %get-tuple-element.1667), channel_id=1, source_target_pairs={{1,0},{2,1},{3,2},{5,4},{6,5},{7,6},{9,8},{10,9},{11,10},{13,12},{... | collective-permute-start | bytes 393224 | tf_op jit(solution)/shard_map/while/body/eval_jaxpr/ppermute | solution.py:16
  1178.1 38.3 %collective-permute-start.2 = (bf16[128,512]{1,0:T(8,128)(2,1)}, bf16[128,512]{1,0:T(8,128)(2,1)}, u32[]{:S(2)}, u32[]{:S(2)}) collective-permute-start(bf16[128,512]{1,0:T(8,128)(2,1)} %fusion.355), channel_id=1, source_target_pairs={{1,0},{2,1},{3,2},{5,4},{6,5},{7,6},{9,8},{10,9},{11,10},{13,12},{... | collective-permute-start | bytes 393224 | tf_op jit(solution)/shard_map/while/body/eval_jaxpr/ppermute | solution.py:16
  1182.0 34.4 %collective-permute-start.3 = (bf16[128,512]{1,0:T(8,128)(2,1)}, bf16[128,512]{1,0:T(8,128)(2,1)}, u32[]{:S(2)}, u32[]{:S(2)}) collective-permute-start(bf16[128,512]{1,0:T(8,128)(2,1)} %get-tuple-element.1667), channel_id=1, source_target_pairs={{1,0},{2,1},{3,2},{5,4},{6,5},{7,6},{9,8},{10,9},{11,10},{13,12},{... | collective-permute-start | bytes 393224 | tf_op jit(solution)/shard_map/while/body/eval_jaxpr/ppermute | solution.py:16
  1270.4 38.8 %collective-permute-start.2 = (bf16[128,512]{1,0:T(8,128)(2,1)}, bf16[128,512]{1,0:T(8,128)(2,1)}, u32[]{:S(2)}, u32[]{:S(2)}) collective-permute-start(bf16[128,512]{1,0:T(8,128)(2,1)} %fusion.355), channel_id=1, source_target_pairs={{1,0},{2,1},{3,2},{5,4},{6,5},{7,6},{9,8},{10,9},{11,10},{13,12},{... | collective-permute-start | bytes 393224 | tf_op jit(solution)/shard_map/while/body/eval_jaxpr/ppermute | solution.py:16
  1274.8 34.4 %collective-permute-start.3 = (bf16[128,512]{1,0:T(8,128)(2,1)}, bf16[128,512]{1,0:T(8,128)(2,1)}, u32[]{:S(2)}, u32[]{:S(2)}) collective-permute-start(bf16[128,512]{1,0:T(8,128)(2,1)} %get-tuple-element.1667), channel_id=1, source_target_pairs={{1,0},{2,1},{3,2},{5,4},{6,5},{7,6},{9,8},{10,9},{11,10},{13,12},{... | collective-permute-start | bytes 393224 | tf_op jit(solution)/shard_map/while/body/eval_jaxpr/ppermute | solution.py:16
  1361.7 38.3 %collective-permute-start.2 = (bf16[128,512]{1,0:T(8,128)(2,1)}, bf16[128,512]{1,0:T(8,128)(2,1)}, u32[]{:S(2)}, u32[]{:S(2)}) collective-permute-start(bf16[128,512]{1,0:T(8,128)(2,1)} %fusion.355), channel_id=1, source_target_pairs={{1,0},{2,1},{3,2},{5,4},{6,5},{7,6},{9,8},{10,9},{11,10},{13,12},{... | collective-permute-start | bytes 393224 | tf_op jit(solution)/shard_map/while/body/eval_jaxpr/ppermute | solution.py:16
  1365.7 34.4 %collective-permute-start.3 = (bf16[128,512]{1,0:T(8,128)(2,1)}, bf16[128,512]{1,0:T(8,128)(2,1)}, u32[]{:S(2)}, u32[]{:S(2)}) collective-permute-start(bf16[128,512]{1,0:T(8,128)(2,1)} %get-tuple-element.1667), channel_id=1, source_target_pairs={{1,0},{2,1},{3,2},{5,4},{6,5},{7,6},{9,8},{10,9},{11,10},{13,12},{... | collective-permute-start | bytes 393224 | tf_op jit(solution)/shard_map/while/body/eval_jaxpr/ppermute | solution.py:16
  1454.1 38.8 %collective-permute-start.2 = (bf16[128,512]{1,0:T(8,128)(2,1)}, bf16[128,512]{1,0:T(8,128)(2,1)}, u32[]{:S(2)}, u32[]{:S(2)}) collective-permute-start(bf16[128,512]{1,0:T(8,128)(2,1)} %fusion.355), channel_id=1, source_target_pairs={{1,0},{2,1},{3,2},{5,4},{6,5},{7,6},{9,8},{10,9},{11,10},{13,12},{... | collective-permute-start | bytes 393224 | tf_op jit(solution)/shard_map/while/body/eval_jaxpr/ppermute | solution.py:16
  1458.5 34.4 %collective-permute-start.3 = (bf16[128,512]{1,0:T(8,128)(2,1)}, bf16[128,512]{1,0:T(8,128)(2,1)}, u32[]{:S(2)}, u32[]{:S(2)}) collective-permute-start(bf16[128,512]{1,0:T(8,128)(2,1)} %get-tuple-element.1667), channel_id=1, source_target_pairs={{1,0},{2,1},{3,2},{5,4},{6,5},{7,6},{9,8},{10,9},{11,10},{13,12},{... | collective-permute-start | bytes 393224 | tf_op jit(solution)/shard_map/while/body/eval_jaxpr/ppermute | solution.py:16
  1545.4 38.3 %collective-permute-start.2 = (bf16[128,512]{1,0:T(8,128)(2,1)}, bf16[128,512]{1,0:T(8,128)(2,1)}, u32[]{:S(2)}, u32[]{:S(2)}) collective-permute-start(bf16[128,512]{1,0:T(8,128)(2,1)} %fusion.355), channel_id=1, source_target_pairs={{1,0},{2,1},{3,2},{5,4},{6,5},{7,6},{9,8},{10,9},{11,10},{13,12},{... | collective-permute-start | bytes 393224 | tf_op jit(solution)/shard_map/while/body/eval_jaxpr/ppermute | solution.py:16
  1549.3 34.4 %collective-permute-start.3 = (bf16[128,512]{1,0:T(8,128)(2,1)}, bf16[128,512]{1,0:T(8,128)(2,1)}, u32[]{:S(2)}, u32[]{:S(2)}) collective-permute-start(bf16[128,512]{1,0:T(8,128)(2,1)} %get-tuple-element.1667), channel_id=1, source_target_pairs={{1,0},{2,1},{3,2},{5,4},{6,5},{7,6},{9,8},{10,9},{11,10},{13,12},{... | collective-permute-start | bytes 393224 | tf_op jit(solution)/shard_map/while/body/eval_jaxpr/ppermute | solution.py:16
  1637.7 38.8 %collective-permute-start.2 = (bf16[128,512]{1,0:T(8,128)(2,1)}, bf16[128,512]{1,0:T(8,128)(2,1)}, u32[]{:S(2)}, u32[]{:S(2)}) collective-permute-start(bf16[128,512]{1,0:T(8,128)(2,1)} %fusion.355), channel_id=1, source_target_pairs={{1,0},{2,1},{3,2},{5,4},{6,5},{7,6},{9,8},{10,9},{11,10},{13,12},{... | collective-permute-start | bytes 393224 | tf_op jit(solution)/shard_map/while/body/eval_jaxpr/ppermute | solution.py:16
  1642.1 34.4 %collective-permute-start.3 = (bf16[128,512]{1,0:T(8,128)(2,1)}, bf16[128,512]{1,0:T(8,128)(2,1)}, u32[]{:S(2)}, u32[]{:S(2)}) collective-permute-start(bf16[128,512]{1,0:T(8,128)(2,1)} %get-tuple-element.1667), channel_id=1, source_target_pairs={{1,0},{2,1},{3,2},{5,4},{6,5},{7,6},{9,8},{10,9},{11,10},{13,12},{... | collective-permute-start | bytes 393224 | tf_op jit(solution)/shard_map/while/body/eval_jaxpr/ppermute | solution.py:16
  1729.1 38.3 %collective-permute-start.2 = (bf16[128,512]{1,0:T(8,128)(2,1)}, bf16[128,512]{1,0:T(8,128)(2,1)}, u32[]{:S(2)}, u32[]{:S(2)}) collective-permute-start(bf16[128,512]{1,0:T(8,128)(2,1)} %fusion.355), channel_id=1, source_target_pairs={{1,0},{2,1},{3,2},{5,4},{6,5},{7,6},{9,8},{10,9},{11,10},{13,12},{... | collective-permute-start | bytes 393224 | tf_op jit(solution)/shard_map/while/body/eval_jaxpr/ppermute | solution.py:16
  1733.0 34.4 %collective-permute-start.3 = (bf16[128,512]{1,0:T(8,128)(2,1)}, bf16[128,512]{1,0:T(8,128)(2,1)}, u32[]{:S(2)}, u32[]{:S(2)}) collective-permute-start(bf16[128,512]{1,0:T(8,128)(2,1)} %get-tuple-element.1667), channel_id=1, source_target_pairs={{1,0},{2,1},{3,2},{5,4},{6,5},{7,6},{9,8},{10,9},{11,10},{13,12},{... | collective-permute-start | bytes 393224 | tf_op jit(solution)/shard_map/while/body/eval_jaxpr/ppermute | solution.py:16
  1821.4 38.8 %collective-permute-start.2 = (bf16[128,512]{1,0:T(8,128)(2,1)}, bf16[128,512]{1,0:T(8,128)(2,1)}, u32[]{:S(2)}, u32[]{:S(2)}) collective-permute-start(bf16[128,512]{1,0:T(8,128)(2,1)} %fusion.355), channel_id=1, source_target_pairs={{1,0},{2,1},{3,2},{5,4},{6,5},{7,6},{9,8},{10,9},{11,10},{13,12},{... | collective-permute-start | bytes 393224 | tf_op jit(solution)/shard_map/while/body/eval_jaxpr/ppermute | solution.py:16
  1825.8 34.4 %collective-permute-start.3 = (bf16[128,512]{1,0:T(8,128)(2,1)}, bf16[128,512]{1,0:T(8,128)(2,1)}, u32[]{:S(2)}, u32[]{:S(2)}) collective-permute-start(bf16[128,512]{1,0:T(8,128)(2,1)} %get-tuple-element.1667), channel_id=1, source_target_pairs={{1,0},{2,1},{3,2},{5,4},{6,5},{7,6},{9,8},{10,9},{11,10},{13,12},{... | collective-permute-start | bytes 393224 | tf_op jit(solution)/shard_map/while/body/eval_jaxpr/ppermute | solution.py:16
  1863.9 40.1 %copy-start.55 = (s32[1024,24]{0,1:T(8,128)S(1)}, s32[1024,24]{0,1:T(8,128)}, u32[]{:S(2)}) copy-start(s32[1024,24]{0,1:T(8,128)} %param.62) | copy-start | bytes 294916
  1863.9 119.9 %reduce-scatter.6.cloned.1.call-start = ((), (), s32[]{:S(2)}) async-start(), calls=%async_computation.4 | async-start | bytes 655360 | tf_op jit(solution)/shard_map/reduce_scatter | solution.py:321
  1866.1 194.3 %all-reduce.9.cloned.1.call-start = ((), (), s32[]{:S(2)}) async-start(), calls=%async_computation.6 | async-start | bytes 786432 | tf_op jit(solution)/shard_map/psum | solution.py:337
  1911.9 183.5 %reduce-scatter.4.cloned.1.call-start = ((), (), s32[]{:S(2)}) async-start(), calls=%async_computation.3 | async-start | bytes 2621440 | tf_op jit(solution)/shard_map/reduce_scatter | solution.py:320
  1913.7 755.1 %all-reduce.11.cloned.1.call-start = ((), (), s32[]{:S(2)}) async-start(), calls=%async_computation.7 | async-start | bytes 37748736 | tf_op jit(solution)/shard_map/psum | solution.py:310
  1913.8 40.4 %copy-start.41 = (f32[3,512]{1,0:T(4,128)S(1)}, f32[3,512]{1,0:T(4,128)}, u32[]{:S(2)}) copy-start(f32[3,512]{1,0:T(4,128)} %get-tuple-element.863) | copy-start | bytes 18436
  1913.8 40.4 %copy-start.56 = (f32[3,512]{1,0:T(4,128)S(1)}, f32[3,512]{1,0:T(4,128)}, u32[]{:S(2)}) copy-start(f32[3,512]{1,0:T(4,128)} %get-tuple-element.1120) | copy-start | bytes 18436
  1913.8 40.6 %copy-start.33 = (f32[3,1024]{1,0:T(4,128)S(1)}, f32[3,1024]{1,0:T(4,128)}, u32[]{:S(2)}) copy-start(f32[3,1024]{1,0:T(4,128)} %get-tuple-element.865) | copy-start | bytes 36868
  1913.8 40.6 %copy-start.44 = (f32[3,512]{1,0:T(4,128)S(1)}, f32[3,512]{1,0:T(4,128)}, u32[]{:S(2)}) copy-start(f32[3,512]{1,0:T(4,128)} %get-tuple-element.867) | copy-start | bytes 18436
  (626 other events, 3685.6 us)
Sparse Core Ops, SparseCore 0:
  1864.1 38.7 reduce-scatter.7
  1906.1 21.6 reduce-scatter.5
  1933.6 126.7 all-reduce.8
  2064.1 31.2 reduce-scatter.3
  2100.1 568.6 all-reduce.10
where the time goes:
time: 2710 us; the launch traced here: 2690 us
  waiting for transfers between devices  722 us (27%)
  matrix products  593 us (22%)
  blocking collectives  562 us (21%)
  other arithmetic  354 us (13%)
  local copies, waits for them, and re-layouts  228 us (8%)
  starting transfers between devices  193 us (7%)
    psum x1, waiting for transfers between devices, on_device(): lax.psum((segment_store[0], segment_store[1], segment_store[2], segment_s...  573 us
    ppermute x44, starting transfers between devices, passed_along(): return lax.ppermute(value, axis, pairs)  193 us
    psum x11, blocking collectives, moments(): total_sum = lax.psum(jnp.sum(source, axis=0), 'dp')  173 us
    psum x11, blocking collectives, backward_tick(): lax.psum((local_sum, local_cross_term), 'dp')  169 us
    dot_general x33, matrix products, weight_terms(): lax.dot_general(gate_input, grad_gate, contract, preferred_element_type=j...  165 us
    psum x11, blocking collectives, moments(): lax.psum(jnp.sum(centred * centred, axis=0), 'dp') / normalized_rows  151 us
    dot_general x66, matrix products, gated_forward(): jnp.dot(cand_input, w_cand, preferred_element_type=jnp.float32) + b_cand  141 us
    another operation x99, other arithmetic  114 us
  transfers between devices with their start and end apart: 49, of which 4 were waited for; matrix products, arithmetic and copies ran while one was open for 18% of the time, Pallas kernels for 0%

commit v1 on v0

v1 whole, which is shorter than its diff:
```python
import jax
import jax.numpy as jnp
from jax import lax
from jax.sharding import PartitionSpec as P

MB = 8
ROWS_MB = 128
EPS = 1e-05
BF = jnp.bfloat16
F32 = jnp.float32


def feature_share(logits, allow):
    allowed = allow > 0
    largest = jnp.max(jnp.where(allowed, logits, -1e30), axis=-1, keepdims=True)
    raised = jnp.where(allowed, jnp.exp(jnp.where(allowed, logits - largest, 0.0)), 0.0)
    return raised / jnp.sum(raised, axis=-1, keepdims=True)


def core_swap(value):
    return lax.ppermute(value, "pipe", [(i, i ^ 1) for i in range(lax.axis_size("pipe"))])


def to_layer(value, up):
    half = lax.axis_size("pipe") // 2
    pairs = [(i, i + half) if up else (i + half, i) for i in range(half)]
    return lax.ppermute(value, "pipe", pairs)


def dp_swap(value, step):
    return lax.ppermute(value, "dp", [(i, i ^ step) for i in range(lax.axis_size("dp"))])


def dp_moments(source, count):
    mean = jnp.mean(source, axis=1)
    centred = source - mean[:, None, :]
    spread = jnp.sum(centred * centred, axis=1)
    step, held = 1, count
    while step < lax.axis_size("dp"):
        other_mean, other_spread = dp_swap((mean, spread), step)
        gap = mean - other_mean
        spread = spread + other_spread + gap * gap * (0.5 * held)
        mean = 0.5 * (mean + other_mean)
        held, step = held * 2, step * 2
    return mean, lax.rsqrt(spread / held + EPS)


def dp_total(value):
    step = 1
    while step < lax.axis_size("dp"):
        value = value + dp_swap(value, step)
        step *= 2
    return value


def rounded(value):
    return lax.reduce_precision(value, 8, 7)


def dot(a, b, dims):
    return lax.dot_general(a, b, ((dims[0], dims[1]), ((), ())), preferred_element_type=F32)


def layer_forward(x, scales, wg, bg, wc, bc):
    width = x.shape[1]
    h = jnp.zeros_like(x)
    kept = []
    for k in range(wg.shape[0]):
        if k == wg.shape[0] // 2:
            h, x = rounded(h), rounded(x)
        m = (x * scales[k]).astype(BF)
        hb = h.astype(BF)
        pre = dot(jnp.concatenate([hb, m], 1), wg[k], ((1,), (0,))) + bg[k]
        z, r = jax.nn.sigmoid(pre[:, :width]), jax.nn.sigmoid(pre[:, width:])
        rh = (r * h).astype(BF)
        c = jnp.tanh(dot(jnp.concatenate([rh, m], 1), wc[k], ((1,), (0,))) + bc[k])
        kept.append((h, z, r, c, hb, m, rh, x))
        h = (1.0 - z) * h + z * c
    return h, kept


def layer_backward(g, kept, scales, wg, wc):
    width = g.shape[1]
    gx = jnp.zeros_like(g)
    gates, cands, gscales = [], [], []
    count = wg.shape[0]
    for k in reversed(range(count)):
        h, z, r, c, hb, m, rh, x = kept[k]
        gc = (g * z * (1.0 - c * c)).astype(BF)
        back_c = dot(gc, wc[k], ((1,), (1,)))
        reset_h = back_c[:, :width]
        gg = jnp.concatenate([g * (c - h) * z * (1.0 - z), reset_h * h * r * (1.0 - r)], 1).astype(BF)
        back_g = dot(gg, wg[k], ((1,), (1,)))
        g = g * (1.0 - z) + reset_h * r + back_g[:, :width]
        gm = back_c[:, width:] + back_g[:, width:]
        gscales.append(jnp.sum(gm * x, axis=0))
        gx = gx + gm * scales[k]
        if k == count // 2:
            g, gx = rounded(g), rounded(gx)
        gates.append(gg)
        cands.append(gc)
    return gx, gates[::-1], cands[::-1], jnp.stack(gscales[::-1])


def on_device(numeric, categories, cardinalities, embed_table, bn_gain, bn_bias, mask_logits,
              feature_allow, gate_weight, gate_bias, cand_weight, cand_bias, out_grad):
    rank = lax.axis_index("pipe")
    core = rank % 2
    first_core = core == 0
    top = rank >= lax.axis_size("pipe") // 2
    width = out_grad.shape[1]
    numeric_width = numeric.shape[1]
    columns, levels, embed_width = embed_table.shape
    batches = MB // 2
    rows = batches * ROWS_MB
    counted = ROWS_MB * lax.axis_size("dp")

    def my_rows(array):
        return lax.dynamic_slice_in_dim(array, core * rows, rows, 0)

    def by_batch(array):
        return array.reshape(batches, ROWS_MB, array.shape[-1])

    shares = feature_share(mask_logits, feature_allow)
    own = (width * shares, gate_weight, gate_bias, cand_weight, cand_bias)
    others = core_swap(own)
    low = [jnp.where(first_core, a, b) for a, b in zip(own, others)]
    high = [jnp.where(first_core, b, a) for a, b in zip(own, others)]
    scales, wg, bg, wc, bc = [jnp.concatenate([a, b], 0) for a, b in zip(low, high)]

    cats = my_rows(categories)
    onehot = (cats[:, :, None] == jnp.arange(levels, dtype=jnp.int32)) & (
        jnp.arange(levels, dtype=jnp.int32) < cardinalities[:, None])
    onehot = onehot.astype(BF)
    embedded = jnp.einsum("rcv,cve->rce", onehot, embed_table, preferred_element_type=F32)
    source1 = jnp.concatenate([my_rows(numeric), embedded.reshape(rows, columns * embed_width)], 1)

    def norm(source, layer):
        mean, spread = dp_moments(by_batch(source), ROWS_MB)
        xhat = (by_batch(source) - mean[:, None]) * spread[:, None]
        return xhat, spread, (xhat * bn_gain[layer] + bn_bias[layer]).reshape(rows, width)

    def norm_back(g, xhat, spread, layer):
        g = by_batch(g)
        sums = jnp.stack([jnp.sum(g, axis=1), jnp.sum(g * xhat, axis=1)])
        totals = dp_total(sums) / counted
        back = bn_gain[layer] * spread[:, None] * (g - totals[0][:, None] - xhat * totals[1][:, None])
        return back.reshape(rows, width), jnp.sum(sums, axis=1)

    xhat1, spread1, x1 = norm(source1, 0)
    h1, kept1 = layer_forward(x1, scales, wg, bg, wc, bc)
    source2 = to_layer(h1.astype(BF), True).astype(F32)
    xhat2, spread2, x2 = norm(source2, 1)
    h2, kept2 = layer_forward(x2, scales, wg, bg, wc, bc)
    gx2, gates2, cands2, gscale2 = layer_backward(my_rows(out_grad), kept2, scales, wg, wc)
    back2, sums2 = norm_back(gx2, xhat2, spread2, 1)
    g1 = to_layer(back2.astype(BF), False).astype(F32)
    gx1, gates1, cands1, gscale1 = layer_backward(g1, kept1, scales, wg, wc)
    back1, sums1 = norm_back(gx1, xhat1, spread1, 0)

    def pick(a, b):
        return jnp.where(top, a, b)

    gate_grads, cand_grads, gate_sums, cand_sums = [], [], [], []
    for k in range(wg.shape[0]):
        gg, gc = pick(gates2[k], gates1[k]), pick(cands2[k], cands1[k])
        hb, m, rh = [pick(kept2[k][i], kept1[k][i]) for i in (4, 5, 6)]
        gate_grads.append(dot(jnp.concatenate([hb, m], 1), gg, ((0,), (0,))))
        cand_grads.append(dot(jnp.concatenate([rh, m], 1), gc, ((0,), (0,))))
        gate_sums.append(jnp.sum(gg.astype(F32), axis=0))
        cand_sums.append(jnp.sum(gc.astype(F32), axis=0))

    def to_owner(stacked, dtype):
        half = len(stacked) // 2
        a, b = jnp.stack(stacked[:half]), jnp.stack(stacked[half:])
        sent = jnp.where(first_core, b, a).astype(dtype)
        return jnp.where(first_core, a, b) + core_swap(sent).astype(F32)

    gate_w = to_owner(gate_grads, BF).astype(BF)
    cand_w = to_owner(cand_grads, BF).astype(BF)
    gate_b, cand_b = to_owner(gate_sums, F32), to_owner(cand_sums, F32)
    gscale = pick(gscale2, gscale1)
    gscale = to_owner([gscale[k] for k in range(gscale.shape[0])], F32)
    gate_w, cand_w = lax.psum((gate_w, cand_w), "dp")
    gate_b, cand_b, gscale = lax.psum((gate_b, cand_b, gscale), "dp")
    scaled = width * gscale
    logit = shares * (scaled - jnp.sum(shares * scaled, axis=-1, keepdims=True))

    gemb = back1[:, numeric_width:].astype(BF).reshape(rows, columns, embed_width)
    table = jnp.einsum("rcv,rce->cve", onehot, gemb, preferred_element_type=F32)
    table = jnp.where(top, 0.0, table)
    sums = jnp.stack([jnp.where(top, 0.0, sums1), jnp.where(top, sums2, 0.0)], axis=1)
    table, sums = lax.psum((table, sums), ("dp", "pipe"))

    def to_columns(mine, source_top):
        half = mine.shape[1] // 2
        share = half // 2
        pieces = mine.reshape(rows, 2, 2, share)
        kept = jnp.where(first_core, pieces[:, :, 0], pieces[:, :, 1])
        sent = jnp.where(first_core, pieces[:, :, 1], pieces[:, :, 0])
        got = core_swap(sent)
        both = jnp.where(first_core, jnp.stack([kept, got]), jnp.stack([got, kept]))
        both = both.reshape(2 * rows, 2, share)
        if source_top:
            return jnp.where(top, both[:, 1], to_layer(both[:, 0], False))
        return jnp.where(top, to_layer(both[:, 1], True), both[:, 0])

    block_out = to_columns(h2, True)
    numeric_grad = to_columns(back1[:, :numeric_width], False)
    return (block_out, numeric_grad, table, sums[1], sums[0], logit,
            gate_w.astype(F32), gate_b, cand_w.astype(F32), cand_b)


def solution(mesh):
    in_specs = (P("dp", None), P("dp", None), P(), P(), P(), P(), P("pipe", None), P("pipe", None),
                P("pipe", None, None), P("pipe", None), P("pipe", None, None), P("pipe", None),
                P("dp", None))
    out_specs = (P("dp", "pipe"), P("dp", "pipe"), P(), P(), P(), P("pipe", None),
                 P("pipe", None, None), P("pipe", None), P("pipe", None, None), P("pipe", None))
    return jax.shard_map(on_device, mesh=mesh, in_specs=in_specs, out_specs=out_specs, check_vma=False)
```

time: 2710 us -> 748 us (0.28)
  blocking collectives: 562 us -> 77.8 us
  matrix products: 593 us -> 109 us
  waiting for transfers between devices: 722 us -> 304 us
  other arithmetic: 354 us -> 143 us
  local copies, waits for them, and re-layouts: 228 us -> 42.2 us
  starting transfers between devices: 193 us -> 45.2 us
    psum x35 -> x2, blocking collectives: 562 us -> 77.8 us  [the longest x1 47.7 us: on_device(): table, sums = lax.psum((table, sums), ('dp', 'pipe'))]
    dot_general x276 -> x62, matrix products: 593 us -> 109 us  [the longest x60 99.2 us: dot(): lax.dot_general(a, b, ((dims[0], dims[1]), ((), ())), preferred_element_t...]
    psum x2, waiting for transfers between devices: 650 us -> 261 us  [the longest x1 142 us: on_device(): gate_w, cand_w = lax.psum((gate_w, cand_w), 'dp')]
    ppermute x44 -> x34, starting transfers between devices: 193 us -> 44.7 us  [the longest x18 20.2 us: dp_swap(): lax.ppermute(value, 'dp', [(i, i ^ step) for i in range(lax.axis_size('dp...]
    another operation x110 -> x20, other arithmetic: 115 us -> 23.1 us
    scatter x44 -> x0, other arithmetic: 89.3 us -> none  [stored_at(): store.at[batch_position]]
    dynamic_slice x78 -> x2, local copies, waits for them, and re-layouts: 79.2 us -> 0.87 us  [my_rows(): return lax.dynamic_slice_in_dim(array, core * rows, rows, 0)]
    reduce_scatter x3 -> x0, waiting for transfers between devices: 71.6 us -> none  [the longest x1 36.6 us: on_device(): lax.psum_scatter(embed_terms, 'pipe', scatter_dimension=1, tiled=True)]
  transfers between devices with their start and end apart: 49 -> 36, of which waited for: 4 -> 20; matrix products, arithmetic and copies ran while one was open for 18% -> 15% of each run, Pallas kernels for 0% -> 0%
where the time goes in v1:
time: 748 us; the launch traced here: 739 us
  waiting for transfers between devices  304 us (41%)
  other arithmetic  143 us (19%)
  matrix products  109 us (15%)
  blocking collectives  77.8 us (10%)
  starting transfers between devices  45.2 us (6%)
  local copies, waits for them, and re-layouts  42.2 us (6%)
  between operations  17.4 us (2%)
    psum x1, waiting for transfers between devices, on_device(): gate_w, cand_w = lax.psum((gate_w, cand_w), 'dp')  142 us
    psum x1, waiting for transfers between devices, on_device(): table, sums = lax.psum((table, sums), ('dp', 'pipe'))  119 us
    dot_general x60, matrix products, dot(): lax.dot_general(a, b, ((dims[0], dims[1]), ((), ())), preferred_element_t...  99.2 us
    psum x1, blocking collectives, on_device(): table, sums = lax.psum((table, sums), ('dp', 'pipe'))  47.7 us
    psum x1, blocking collectives, on_device(): gate_b, cand_b, gscale = lax.psum((gate_b, cand_b, gscale), 'dp')  30.1 us
    unnamed x489, local copies, waits for them, and re-layouts  28.7 us
    another operation x17, other arithmetic  23 us
    ppermute x18, waiting for transfers between devices, dp_swap(): lax.ppermute(value, 'dp', [(i, i ^ step) for i in range(lax.axis_size('dp...  21.3 us
  transfers between devices with their start and end apart: 36, of which 20 were waited for; matrix products, arithmetic and copies ran while one was open for 15% of the time, Pallas kernels for 0%

profile of v1, /device:TPU:1, one launch (start us, length us, event | category | flops | bytes accessed | tf_op | source)
XLA Modules:
  0.0 739.3 jit_solution(4428756920626671875)
XLA Ops:
  12.7 5.3 fusion.3
  19.1 2.4 collective-permute-start
  21.7 2.2 multiply_reduce_fusion.10
  25.2 2.4 collective-permute-done.3
  31.5 2.4 collective-permute-start.5
  35.0 2.3 collective-permute-done.2
  40.6 3.1 broadcast_select_fusion.2
  44.2 4.7 broadcast_select_fusion
  50.5 2.7 fusion.279
  56.1 1.9 fusion.278
  59.7 1.9 fusion.277
  63.2 1.9 fusion.276
  66.8 1.9 fusion.275
  72.2 3.7 collective-permute-start.11
  75.9 6.6 collective-permute-done.11
  89.2 2.3 collective-permute-start.14
  93.6 2.8 broadcast_select_fusion.33
  99.8 2.2 broadcast_select_fusion.32
  104.4 2.2 broadcast_select_fusion.30
  109.1 2.2 broadcast_select_fusion.28
  114.8 2.1 broadcast_select_fusion.26
  119.5 2.3 broadcast_select_fusion.24
  124.9 2.3 multiply_convert_fusion.30
  129.2 2.6 fusion.30
  131.9 3.0 multiply_convert_fusion.27
  137.9 4.7 fusion.28
  142.6 3.5 multiply_convert_fusion.24
  149.9 4.6 fusion.26
  154.5 3.2 multiply_convert_fusion.21
  161.5 4.0 multiply_convert_fusion.18
  169.3 2.7 fusion.22
  172.0 2.2 multiply_convert_fusion.15
  175.8 4.6 bitcast_reduce_fusion
  187.2 2.0 collective-permute-done.22
  191.2 8.6 %collective-permute-done.23 = bf16[512,512]{1,0:T(8,128)(2,1)S(1)} collective-permute-done((bf16[512,512]{1,0:T(8,128)(2,1)S(1)}, bf16[512,512]{1,0:T(8,128)(2,1)S(1)}, u32[]{:S(2)}, u32[]{:S(2)}) %collective-permute-start.23) | collective-permute-done | bytes 524320 | tf_op jit(solution)/shard_map/ppermute | solution.py:27
  201.9 3.4 fusion.29
  219.8 2.4 multiply_reduce_fusion.1
  246.8 4.0 select_convert_fusion
  250.8 12.6 %collective-permute-start.30 = (bf16[3,1024,1024]{2,1,0:T(8,128)(2,1)}, bf16[3,1024,1024]{2,1,0:T(8,128)(2,1)}, u32[]{:S(2)}, u32[]{:S(2)}) collective-permute-start(bf16[3,1024,1024]{2,1,0:T(8,128)(2,1)} %select_convert_fusion), channel_id=1, source_target_pairs={{0,1},{1,0},{2,3},{3,2},{4,5},{5,4},{6,7},{7,6},{8,9},{9,8},{10,11... | collective-permute-start | bytes 18874376 | tf_op jit(solution)/shard_map/ppermute | solution.py:21
  269.4 2.1 convolution_bitcast_fusion.10
  271.5 2.1 convolution_bitcast_fusion.11
  273.7 4.0 select_convert_fusion.1
  277.7 6.0 collective-permute-done.32
  283.7 5.8 add_convert_fusion.1
  289.5 7.9 %add_convert_fusion = bf16[3,1024,1024]{2,1,0:T(8,128)(2,1)} fusion(bf16[3,1024,1024]{2,1,0:T(8,128)(2,1)} %collective-permute-done.30, f32[1,1024,1024]{2,1,0:T(8,128)S(1)} %convolution_bitcast_fusion, f32[1,1024,1024]{2,1,0:T(8,128)S(1)} %convolution_bitcast_fusion.1, f32[1,1024,1024]{2,1,0:T(8,128)S(1)} %convolution_bitcast_fusion.2, ...), kind=kLoop, calls=%fused_computation.2 | loop fusion | flops 25165824 | bytes 37748736 | tf_op jit(solution)/shard_map/convert_element_type | solution.py:179
  300.3 4.0 fusion.280
  306.2 5.5 multiply_reduce_fusion.6
  313.8 2.0 maximum_select_fusion
  319.2 2.0 convert_reduce_fusion
  323.1 2.0 convert_reduce_fusion.2
  325.1 2.0 convert_reduce_fusion.3
  331.6 5.2 bitcast_reduce_fusion.2
  336.8 2.6 copy.222
  339.4 9.8 %multiply_reduce_fusion.9 = f32[4,512]{0,1:T(8,128)} fusion(f32[4,128,512]{1,0,2:T(4,128)} %copy.222, f32[4,512]{0,1:T(8,128)} %copy.204, f32[4,512]{0,1:T(8,128)} %copy.199, f32[4,128,384]{1,0,2:T(4,128)} %copy-done.38, f32[4,128,128]{1,0,2:T(4,128)S(1)} %copy-done.94), kind=kLoop, calls=%fused_computation.370 | loop fusion | flops 1308672 | bytes 2121728 | tf_op jit(solution)/shard_map/reduce_sum | solution.py:145
  354.9 47.7 %psum.50 = f32[2,2,512]{2,1,0:T(2,128)S(1)} all-reduce(f32[2,2,512]{2,1,0:T(2,128)S(1)} %pad_maximum_fusion.93), channel_id=1, replica_groups=mesh['dp'=8,'pipe'=4] {'dp','pipe'}, use_global_device_ids=true, to_apply=%region_13.14 | all-reduce | flops 2048 | bytes 16384 | tf_op jit(solution)/shard_map/psum | solution.py:193
  404.6 5.0 collective-permute-done.26
  409.7 4.3 multiply_reduce_fusion
  415.0 4.9 fusion.31
  420.2 30.1 %all-reduce.3 = (f32[3,512]{1,0:T(4,128)S(1)}, f32[3,1024]{1,0:T(4,128)}, f32[3,512]{1,0:T(4,128)}) all-reduce(f32[3,512]{1,0:T(4,128)S(1)} %select_add_fusion.2, f32[3,1024]{1,0:T(4,128)S(1)} %select_add_fusion, f32[3,512]{1,0:T(4,128)S(1)} %select_add_fusion.1), channel_id=1, replica_groups=mesh['dp'=8,'pipe'=4] {'dp'}, use_global_device_ids=true, to_apply=%region_26.27 | all-reduce | flops 6144 | bytes 49152 | tf_op jit(solution)/shard_map/psum | solution.py:185
  455.0 1.9 fusion.208
  457.0 142.0 %all-reduce.10.cloned.1.call-done = (bf16[3,1024,1024]{2,1,0:T(8,128)(2,1)}, bf16[3,1024,512]{2,1,0:T(8,128)(2,1)}) async-done(((bf16[3,1024,1024]{2,1,0:T(8,128)(2,1)}, bf16[3,1024,512]{2,1,0:T(8,128)(2,1)}), (bf16[3,1024,1024]{2,1,0:T(8,128)(2,1)}, bf16[3,1024,512]{2,1,0:T(8,128)(2,1)})) %all-reduce.10.cloned.1.call-update) | async-done | bytes 9437200 | tf_op jit(solution)/shard_map/psum | solution.py:184
  598.9 9.3 %convert_element_type.280 = f32[3,1024,1024]{2,1,0:T(8,128)} convert(bf16[3,1024,1024]{2,1,0:T(8,128)(2,1)} %get-tuple-element.27) | non-fusion elementwise | flops 3145728 | bytes 18874368 | tf_op jit(solution)/shard_map/convert_element_type | solution.py:211
  608.2 3.6 convert_element_type.290
  611.8 118.7 %all-reduce.8.cloned.1.call-done = f32[24,256,16]{1,2,0:T(8,128)} async-done(((f32[24,256,16]{1,2,0:T(8,128)}), f32[24,256,16]{1,2,0:T(8,128)}) %all-reduce.8.cloned.1.call-update) | async-done | bytes 393232 | tf_op jit(solution)/shard_map/psum | solution.py:193
  (710 shorter events, 159.5 us)
Async XLA Ops:
  7.2 591.7 %all-reduce.10.cloned.1.call-start = ((), (), s32[]{:S(2)}) async-start(), calls=%async_computation.1 | async-start | bytes 18874368 | tf_op jit(solution)/shard_map/psum | solution.py:184
  7.2 36.4 %collective-permute-start.7 = (bf16[3,1024,1024]{2,1,0:T(8,128)(2,1)}, bf16[3,1024,1024]{2,1,0:T(8,128)(2,1)}, u32[]{:S(2)}, u32[]{:S(2)}) collective-permute-start(bf16[3,1024,1024]{2,1,0:T(8,128)(2,1)} %param.21), channel_id=1, source_target_pairs={{0,1},{1,0},{2,3},{3,2},{4,5},{5,4},{6,7},{7,6},{8,9},{9,8},{10,11... | collective-permute-start | bytes 18874376 | tf_op jit(solution)/shard_map/ppermute | solution.py:21
  9.9 14.5 %collective-permute-start.6 = (f32[3,512]{1,0:T(4,128)S(1)}, f32[3,512]{1,0:T(4,128)S(1)}, u32[]{:S(2)}, u32[]{:S(2)}) collective-permute-start(f32[3,512]{1,0:T(4,128)S(1)} %get-tuple-element.112), channel_id=1, source_target_pairs={{0,1},{1,0},{2,3},{3,2},{4,5},{5,4},{6,7},{7,6},{8,9},{9,8},{10,11... | collective-permute-start | bytes 18440 | tf_op jit(solution)/shard_map/ppermute | solution.py:21
  10.4 14.7 %collective-permute-start.10 = (f32[3,512]{1,0:T(4,128)}, f32[3,512]{1,0:T(4,128)S(1)}, u32[]{:S(2)}, u32[]{:S(2)}) collective-permute-start(f32[3,512]{1,0:T(4,128)} %param.24), channel_id=1, source_target_pairs={{0,1},{1,0},{2,3},{3,2},{4,5},{5,4},{6,7},{7,6},{8,9},{9,8},{10,11... | collective-permute-start | bytes 18440 | tf_op jit(solution)/shard_map/ppermute | solution.py:21
  10.5 28.8 %collective-permute-start.9 = (bf16[3,1024,512]{2,1,0:T(8,128)(2,1)}, bf16[3,1024,512]{2,1,0:T(8,128)(2,1)}, u32[]{:S(2)}, u32[]{:S(2)}) collective-permute-start(bf16[3,1024,512]{2,1,0:T(8,128)(2,1)} %param.23), channel_id=1, source_target_pairs={{0,1},{1,0},{2,3},{3,2},{4,5},{5,4},{6,7},{7,6},{8,9},{9,8},{10,11... | collective-permute-start | bytes 9437192 | tf_op jit(solution)/shard_map/ppermute | solution.py:21
  10.9 27.3 %copy-start.40 = (f32[512,128]{1,0:T(8,128)}, f32[512,128]{1,0:T(8,128)S(1)}, u32[]{:S(2)}) copy-start(f32[512,128]{1,0:T(8,128)S(1)} %constant_dynamic-slice_fusion.1) | copy-start | bytes 786436
  19.1 6.1 collective-permute-start
  21.7 71.8 %copy-start.208 = (f32[1,512]{1,0:T(1,128)}, f32[1,512]{1,0:T(1,128)S(1)}, u32[]{:S(2)}) copy-start(f32[1,512]{1,0:T(1,128)S(1)} %get-tuple-element.200) | copy-start | bytes 6148
  21.7 71.8 %copy-start.210 = (f32[1,512]{1,0:T(1,128)}, f32[1,512]{1,0:T(1,128)S(1)}, u32[]{:S(2)}) copy-start(f32[1,512]{1,0:T(1,128)S(1)} %get-tuple-element.202) | copy-start | bytes 6148
  24.4 4.8 collective-permute-start.8
  25.1 2.5 collective-permute-start.3
  27.7 2.6 collective-permute-start.4
  29.0 2.5 collective-permute-start.1
  31.5 3.5 collective-permute-start.5
  33.9 3.4 collective-permute-start.2
  38.2 28.6 %copy-start.142 = (bf16[512,512]{1,0:T(8,128)(2,1)}, bf16[512,512]{1,0:T(8,128)(2,1)S(1)}, u32[]{:S(2)}) copy-start(bf16[512,512]{1,0:T(8,128)(2,1)S(1)} %multiply_convert_fusion.44) | copy-start | bytes 1572868
  39.2 20.4 %copy-start.154 = (bf16[512,512]{1,0:T(8,128)(2,1)}, bf16[512,512]{1,0:T(8,128)(2,1)S(1)}, u32[]{:S(2)}) copy-start(bf16[512,512]{1,0:T(8,128)(2,1)S(1)} %get-tuple-element.138) | copy-start | bytes 1572868
  39.2 24.0 %copy-start.156 = (bf16[512,512]{1,0:T(8,128)(2,1)}, bf16[512,512]{1,0:T(8,128)(2,1)S(1)}, u32[]{:S(2)}) copy-start(bf16[512,512]{1,0:T(8,128)(2,1)S(1)} %get-tuple-element.139) | copy-start | bytes 1572868
  39.2 31.1 %copy-start.160 = (bf16[512,512]{1,0:T(8,128)(2,1)}, bf16[512,512]{1,0:T(8,128)(2,1)S(1)}, u32[]{:S(2)}) copy-start(bf16[512,512]{1,0:T(8,128)(2,1)S(1)} %get-tuple-element.141) | copy-start | bytes 1572868
  43.6 26.7 %copy-start.2 = (bf16[3,1024,512]{2,1,0:T(8,128)(2,1)}, bf16[3,1024,512]{2,1,0:T(8,128)(2,1)S(1)}, u32[]{:S(2)}) copy-start(bf16[3,1024,512]{2,1,0:T(8,128)(2,1)S(1)} %get-tuple-element.118) | copy-start | bytes 9437188
  48.9 19.8 %copy-start.51 = (bf16[3,1024,1024]{2,1,0:T(8,128)(2,1)}, bf16[3,1024,1024]{2,1,0:T(8,128)(2,1)S(1)}, u32[]{:S(2)}) copy-start(bf16[3,1024,1024]{2,1,0:T(8,128)(2,1)S(1)} %get-tuple-element.116) | copy-start | bytes 18874372
  72.2 10.2 %collective-permute-start.11 = (bf16[512,512]{1,0:T(8,128)(2,1)S(1)}, bf16[512,512]{1,0:T(8,128)(2,1)S(1)}, u32[]{:S(2)}, u32[]{:S(2)}) collective-permute-start(bf16[512,512]{1,0:T(8,128)(2,1)S(1)} %get-tuple-element.209), channel_id=1, source_target_pairs={{0,2},{1,3},{4,6},{5,7},{8,10},{9,11},{12,14},{13,15},{16,18},{17,... | collective-permute-start | bytes 1572872 | tf_op jit(solution)/shard_map/ppermute | solution.py:27
  83.4 2.6 collective-permute-start.15
  83.7 2.5 collective-permute-start.12
  86.2 2.6 collective-permute-start.16
  86.5 2.5 collective-permute-start.13
  89.0 4.5 collective-permute-start.17
  89.2 4.3 collective-permute-start.14
  93.5 82.2 %copy-start.44 = (bf16[1024,1024]{1,0:T(8,128)(2,1)}, bf16[1024,1024]{1,0:T(8,128)(2,1)S(1)}, u32[]{:S(2)}) copy-start(bf16[1024,1024]{1,0:T(8,128)(2,1)S(1)} %slice_bitcast_fusion.5) | copy-start | bytes 6291460
  96.5 25.3 %copy-start.187 = (bf16[512,512]{1,0:T(8,128)(2,1)}, bf16[512,512]{1,0:T(8,128)(2,1)S(1)}, u32[]{:S(2)}) copy-start(bf16[512,512]{1,0:T(8,128)(2,1)S(1)} %get-tuple-element.155) | copy-start | bytes 1572868
  128.7 47.0 %copy-start.9 = (f32[512,1024]{1,0:T(8,128)}, f32[512,1024]{1,0:T(8,128)S(1)}, u32[]{:S(2)}) copy-start(f32[512,1024]{1,0:T(8,128)S(1)} %fusion.207) | copy-start | bytes 6291460
  136.7 68.6 %copy-start.62 = (bf16[512,512]{1,0:T(8,128)(2,1)}, bf16[512,512]{1,0:T(8,128)(2,1)S(1)}, u32[]{:S(2)}) copy-start(bf16[512,512]{1,0:T(8,128)(2,1)S(1)} %multiply_convert_fusion.28) | copy-start | bytes 1572868
  137.4 38.3 %copy-start.11 = (f32[512,1024]{1,0:T(8,128)}, f32[512,1024]{1,0:T(8,128)S(1)}, u32[]{:S(2)}) copy-start(f32[512,1024]{1,0:T(8,128)S(1)} %fusion.205) | copy-start | bytes 6291460
  148.4 27.3 %copy-start.12 = (f32[512,1024]{1,0:T(8,128)}, f32[512,1024]{1,0:T(8,128)S(1)}, u32[]{:S(2)}) copy-start(f32[512,1024]{1,0:T(8,128)S(1)} %fusion.203) | copy-start | bytes 6291460
  175.8 24.1 %copy-start.43 = (f32[512,512]{1,0:T(8,128)S(1)}, f32[512,512]{1,0:T(8,128)}, u32[]{:S(2)}) copy-start(f32[512,512]{1,0:T(8,128)} %copy-done.42) | copy-start | bytes 3145732
  175.8 24.1 %copy-start.134 = (bf16[512,512]{1,0:T(8,128)(2,1)S(1)}, bf16[512,512]{1,0:T(8,128)(2,1)}, u32[]{:S(2)}) copy-start(bf16[512,512]{1,0:T(8,128)(2,1)} %copy-done.133) | copy-start | bytes 1572868
  175.8 24.1 %copy-start.170 = (f32[512,512]{1,0:T(8,128)S(1)}, f32[512,512]{1,0:T(8,128)}, u32[]{:S(2)}) copy-start(f32[512,512]{1,0:T(8,128)} %get-tuple-element.210) | copy-start | bytes 3145732
  180.4 19.5 %copy-start.35 = (f32[512,1024]{1,0:T(8,128)S(1)}, f32[512,1024]{1,0:T(8,128)}, u32[]{:S(2)}) copy-start(f32[512,1024]{1,0:T(8,128)} %copy-done.34) | copy-start | bytes 6291460
  180.4 2.7 collective-permute-start.20
  183.1 2.7 collective-permute-start.21
  185.7 3.5 collective-permute-start.22
  189.5 10.3 %collective-permute-start.23 = (bf16[512,512]{1,0:T(8,128)(2,1)S(1)}, bf16[512,512]{1,0:T(8,128)(2,1)S(1)}, u32[]{:S(2)}, u32[]{:S(2)}) collective-permute-start(bf16[512,512]{1,0:T(8,128)(2,1)S(1)} %fusion.165), channel_id=1, source_target_pairs={{2,0},{3,1},{6,4},{7,5},{10,8},{11,9},{14,12},{15,13},{18,16},{19,... | collective-permute-start | bytes 1572872 | tf_op jit(solution)/shard_map/ppermute | solution.py:27
  210.3 29.0 %copy-start.100 = (bf16[512,512]{1,0:T(8,128)(2,1)}, bf16[512,512]{1,0:T(8,128)(2,1)S(1)}, u32[]{:S(2)}) copy-start(bf16[512,512]{1,0:T(8,128)(2,1)S(1)} %get-tuple-element.133) | copy-start | bytes 1572868
  210.3 29.0 %copy-start.102 = (bf16[512,512]{1,0:T(8,128)(2,1)}, bf16[512,512]{1,0:T(8,128)(2,1)S(1)}, u32[]{:S(2)}) copy-start(bf16[512,512]{1,0:T(8,128)(2,1)S(1)} %get-tuple-element.134) | copy-start | bytes 1572868
  250.8 38.7 %collective-permute-start.30 = (bf16[3,1024,1024]{2,1,0:T(8,128)(2,1)}, bf16[3,1024,1024]{2,1,0:T(8,128)(2,1)}, u32[]{:S(2)}, u32[]{:S(2)}) collective-permute-start(bf16[3,1024,1024]{2,1,0:T(8,128)(2,1)} %select_convert_fusion), channel_id=1, source_target_pairs={{0,1},{1,0},{2,3},{3,2},{4,5},{5,4},{6,7},{7,6},{8,9},{9,8},{10,11... | collective-permute-start | bytes 18874376 | tf_op jit(solution)/shard_map/ppermute | solution.py:21
  277.7 6.0 collective-permute-start.32
  297.4 433.1 %all-reduce.8.cloned.1.call-start = ((), (), s32[]{:S(2)}) async-start(), calls=%async_computation | async-start | bytes 786432 | tf_op jit(solution)/shard_map/psum | solution.py:193
  304.3 9.5 %collective-permute-start.18 = (f32[512,2,128]{2,1,0:T(2,128)}, f32[512,2,128]{2,1,0:T(2,128)}, u32[]{:S(2)}, u32[]{:S(2)}) collective-permute-start(f32[512,2,128]{2,1,0:T(2,128)} %bitcast.45), channel_id=1, source_target_pairs={{0,1},{1,0},{2,3},{3,2},{4,5},{5,4},{6,7},{7,6},{8,9},{9,8},{10,11... | collective-permute-start | bytes 1572872 | tf_op jit(solution)/shard_map/ppermute | solution.py:21
  311.7 19.9 %copy-start.56 = (f32[512,1024]{1,0:T(8,128)S(1)}, f32[512,1024]{1,0:T(8,128)}, u32[]{:S(2)}) copy-start(f32[512,1024]{1,0:T(8,128)} %copy-done.55) | copy-start | bytes 6291460
  313.8 17.8 %copy-start.53 = (f32[512,1024]{1,0:T(8,128)S(1)}, f32[512,1024]{1,0:T(8,128)}, u32[]{:S(2)}) copy-start(f32[512,1024]{1,0:T(8,128)} %copy-done.52) | copy-start | bytes 6291460
  316.8 138.3 %collective-permute-start.19 = (f32[1024,128]{1,0:T(8,128)}, f32[1024,128]{1,0:T(8,128)}, u32[]{:S(2)}, u32[]{:S(2)}) collective-permute-start(f32[1024,128]{1,0:T(8,128)} %slice_bitcast_fusion.56), channel_id=1, source_target_pairs={{2,0},{3,1},{6,4},{7,5},{10,8},{11,9},{14,12},{15,13},{18,16},{19,... | collective-permute-start | bytes 1572872 | tf_op jit(solution)/shard_map/ppermute | solution.py:27
  318.8 32.7 %collective-permute-start.33 = (f32[3,512]{1,0:T(4,128)}, f32[3,512]{1,0:T(4,128)}, u32[]{:S(2)}, u32[]{:S(2)}) collective-permute-start(f32[3,512]{1,0:T(4,128)} %fusion.214), channel_id=1, source_target_pairs={{0,1},{1,0},{2,3},{3,2},{4,5},{5,4},{6,7},{7,6},{8,9},{9,8},{10,11... | collective-permute-start | bytes 18440 | tf_op jit(solution)/shard_map/ppermute | solution.py:21
  331.4 20.8 %collective-permute-start.31 = (f32[3,1024]{1,0:T(4,128)}, f32[3,1024]{1,0:T(4,128)S(1)}, u32[]{:S(2)}, u32[]{:S(2)}) collective-permute-start(f32[3,1024]{1,0:T(4,128)} %fusion.213), channel_id=1, source_target_pairs={{0,1},{1,0},{2,3},{3,2},{4,5},{5,4},{6,7},{7,6},{8,9},{9,8},{10,11... | collective-permute-start | bytes 36872 | tf_op jit(solution)/shard_map/ppermute | solution.py:21
  339.3 70.3 %copy-start.6 = (f32[512,384]{1,0:T(8,128)S(1)}, f32[512,384]{1,0:T(8,128)}, u32[]{:S(2)}) copy-start(f32[512,384]{1,0:T(8,128)} %copy-done.4) | copy-start | bytes 2359300
  339.3 70.3 %copy-start.207 = (f32[4,512]{1,0:T(4,128)S(1)}, f32[4,512]{1,0:T(4,128)}, u32[]{:S(2)}) copy-start(f32[4,512]{1,0:T(4,128)} %get-tuple-element.85) | copy-start | bytes 24580
  350.2 3.1 collective-permute-start.24
  353.4 49.3 %collective-permute-start.25 = (f32[2,4,512]{2,1,0:T(4,128)S(1)}, f32[2,4,512]{2,1,0:T(4,128)S(1)}, u32[]{:S(2)}, u32[]{:S(2)}) collective-permute-start(f32[2,4,512]{2,1,0:T(4,128)S(1)} %get-tuple-element.159), channel_id=1, source_target_pairs={{0,8},{4,12},{8,0},{12,4},{16,24},{20,28},{24,16},{28,20},{1,9},{5... | collective-permute-start | bytes 49160 | tf_op jit(solution)/shard_map/ppermute | solution.py:31
  402.7 6.9 collective-permute-start.26
  414.2 6.0 collective-permute-start.29
  415.0 35.4 %copy-start.200 = (f32[3,512]{1,0:T(4,128)S(1)}, f32[3,512]{1,0:T(4,128)}, u32[]{:S(2)}) copy-start(f32[3,512]{1,0:T(4,128)} %copy-done.199) | copy-start | bytes 18436
  419.9 35.2 %copy-start.92 = (f32[2,512,2,128]{3,1,0,2:T(8,128)S(1)}, f32[2,512,2,128]{3,1,0,2:T(8,128)}, u32[]{:S(2)}) copy-start(f32[2,512,2,128]{3,1,0,2:T(8,128)} %copy-done.91) | copy-start | bytes 3145732
  419.9 30.6 %collective-permute-start.27 = (f32[512,2,32]{0,2,1:T(8,128)S(1)}, f32[512,2,32]{0,2,1:T(8,128)S(1)}, u32[]{:S(2)}, u32[]{:S(2)}) collective-permute-start(f32[512,2,32]{0,2,1:T(8,128)S(1)} %select_bitcast_fusion.1), channel_id=1, source_target_pairs={{0,1},{1,0},{2,3},{3,2},{4,5},{5,4},{6,7},{7,6},{8,9},{9,8},{10,11... | collective-permute-start | bytes 393224 | tf_op jit(solution)/shard_map/ppermute | solution.py:21
  450.5 3.8 collective-permute-start.28
  608.2 124.1 %copy-start.1 = (f32[1024,128]{1,0:T(8,128)S(1)}, f32[1024,128]{1,0:T(8,128)}, u32[]{:S(2)}) copy-start(f32[1024,128]{1,0:T(8,128)} %param.13) | copy-start | bytes 1572868
  (216 other events, 841.4 us)
Sparse Core Ops, SparseCore 0:
  297.5 301.3 all-reduce.9
  604.8 125.6 all-reduce.7
